TPU v7x, 32 devices: a whole 2x2x4 slice. The times are simulated.
32 devices in a mesh: row: 4 (over y, core), col: 8 (over z, x).
Axes of the slice: x: 2, y: 2, z: 4, core: 2. Of those that a mesh axis runs over, the one named last changes fastest.
Arguments:
- inputs: bfloat16 [32, 128, 512], P('row', 'col'), may hold values from -6 to 6
- cotangent: bfloat16 [32, 128, 512], P('row', 'col'), may hold values from -6 to 6
- first_weight: bfloat16 [512, 256], replicated, may hold values from -0.25 to 0.25
- grouped_weight: bfloat16 [3, 3, 8, 256], replicated, may hold values from -0.75 to 0.75
- third_weight: bfloat16 [256, 512], replicated, may hold values from -0.375 to 0.375
- scale_first: float32 [256], replicated, may hold values from 0.5 to 2
- shift_first: float32 [256], replicated, may hold values from -0.5 to 0.5
- scale_mid: float32 [256], replicated, may hold values from 0.5 to 2
- shift_mid: float32 [256], replicated, may hold values from -0.5 to 0.5
- scale_third: float32 [512], replicated, may hold values from 0.5 to 2
- shift_third: float32 [512], replicated, may hold values from -0.5 to 0.5
Outputs:
- grad_input: bfloat16 [32, 128, 512], P('row', 'col')
- grad_first: float32 [512, 256], replicated
- grad_grouped: float32 [3, 3, 8, 256], replicated
- grad_third: float32 [256, 512], replicated
All inputs are finite; a program needn't handle non-finite values.
Results may differ from a plain program's by a relative error of at most 0.0073.
Values may be sent and summed in bfloat16 or wider, within the bound.
A program may use at most 64 MiB of HBM per device.

v0:
```python
import math

import jax
import jax.numpy as jnp
from jax import lax
from jax.sharding import PartitionSpec as P


def padded_2(cells, sides, width):
    for axis, dim in sides:
        count = lax.axis_size(axis)
        ends = count - 1
        head = lax.slice_in_dim(cells, 0, width, axis=dim)
        tail = lax.slice_in_dim(cells, cells.shape[dim] - width, cells.shape[dim], axis=dim)
        cells = jnp.concatenate(
            [
                lax.ppermute(tail, axis, [(i, (i + 1) % count) for i in range(ends)]),
                cells,
                lax.ppermute(head, axis, [((i + 1) % count, i) for i in range(ends)]),
            ],
            axis=dim,
        )
    return cells


def silu_slope(values):
    logistic = jax.nn.sigmoid(values)
    return logistic * (1.0 + values * (1.0 - logistic))


def block_mask(hidden_dim, width):
    source = lax.broadcasted_iota(jnp.int32, (hidden_dim, hidden_dim), 0) // width
    target = lax.broadcasted_iota(jnp.int32, (hidden_dim, hidden_dim), 1) // width
    return source == target


def dense_kernel(kernel):
    width = kernel.shape[2]
    hidden_dim = kernel.shape[3]
    tiled = jnp.tile(kernel, (1, 1, hidden_dim // width, 1))
    return jnp.where(block_mask(hidden_dim, width)[None, None], tiled, jnp.zeros_like(tiled))


def conv_forward(padded, dense, tile_rows, tile_cols):
    hidden_dim = dense.shape[3]
    total = jnp.zeros((tile_rows * tile_cols, hidden_dim), jnp.float32)
    for row_off in range(3):
        for col_off in range(3):
            window = padded[row_off : row_off + tile_rows, col_off : col_off + tile_cols].reshape(
                tile_rows * tile_cols, hidden_dim
            )
            total = total + jnp.dot(
                window, dense[row_off, col_off], preferred_element_type=jnp.float32
            )
    return total.reshape(tile_rows, tile_cols, hidden_dim)


def conv_backward(err_padded, dense, tile_rows, tile_cols):
    hidden_dim = dense.shape[3]
    total = jnp.zeros((tile_rows * tile_cols, hidden_dim), jnp.float32)
    for row_off in range(3):
        for col_off in range(3):
            window = err_padded[
                2 - row_off : 2 - row_off + tile_rows, 2 - col_off : 2 - col_off + tile_cols
            ].reshape(tile_rows * tile_cols, hidden_dim)
            total = total + contract_cols(window, dense[row_off, col_off])
    return total.reshape(tile_rows, tile_cols, hidden_dim)


def tap_grads(padded_act, err_mid, width):
    tile_rows, tile_cols, hidden_dim = err_mid.shape
    flat_err = err_mid.reshape(tile_rows * tile_cols, hidden_dim)
    keep = block_mask(hidden_dim, width)
    taps = []
    for row_off in range(3):
        for col_off in range(3):
            window = padded_act[
                row_off : row_off + tile_rows, col_off : col_off + tile_cols
            ].reshape(tile_rows * tile_cols, hidden_dim)
            square = jnp.where(keep, contract_rows(window, flat_err), 0.0)
            taps.append(jnp.sum(square.reshape(hidden_dim // width, width, hidden_dim), axis=0))
    return jnp.stack(taps).reshape(3, 3, width, hidden_dim)


def contract_rows(left, right):
    return lax.dot_general(
        left, right, (((0,), (0,)), ((), ())), preferred_element_type=jnp.float32
    )


def contract_cols(left, right):
    return lax.dot_general(
        left, right, (((1,), (1,)), ((), ())), preferred_element_type=jnp.float32
    )


def body(
    inputs,
    cotangent,
    first_weight,
    grouped_weight,
    third_weight,
    scale_first,
    shift_first,
    scale_mid,
    shift_mid,
    scale_third,
    shift_third,
):
    tile_rows, tile_cols, in_chans = inputs.shape
    hidden_dim = first_weight.shape[1]
    width = grouped_weight.shape[2]
    dense = dense_kernel(grouped_weight)
    flat_input = inputs.reshape(tile_rows * tile_cols, in_chans)
    pre_first = (
        jnp.dot(flat_input, first_weight, preferred_element_type=jnp.float32) * scale_first
        + shift_first
    ).reshape(tile_rows, tile_cols, hidden_dim)
    act_first = jax.nn.silu(pre_first).astype(jnp.bfloat16)
    padded_act = padded_2(act_first, (("row", 0), ("col", 1)), 1)
    pre_mid = conv_forward(padded_act, dense, tile_rows, tile_cols) * scale_mid + shift_mid
    act_mid = jax.nn.silu(pre_mid).astype(jnp.bfloat16)
    flat_mid = act_mid.reshape(tile_rows * tile_cols, hidden_dim)
    pre_third = (
        jnp.dot(flat_mid, third_weight, preferred_element_type=jnp.float32) * scale_third
        + shift_third
        + flat_input.astype(jnp.float32)
    )
    back_third = cotangent.reshape(tile_rows * tile_cols, in_chans).astype(
        jnp.float32
    ) * silu_slope(pre_third)
    err_third = (back_third * scale_third).astype(jnp.bfloat16)
    grad_third = contract_rows(flat_mid, err_third)
    back_mid = contract_cols(err_third, third_weight).reshape(tile_rows, tile_cols, hidden_dim)
    err_mid = (back_mid * silu_slope(pre_mid) * scale_mid).astype(jnp.bfloat16)
    err_padded = padded_2(err_mid, (("row", 0), ("col", 1)), 1)
    grad_grouped = tap_grads(padded_act, err_mid, width)
    back_first = conv_backward(err_padded, dense, tile_rows, tile_cols)
    err_first = (
        (back_first * silu_slope(pre_first) * scale_first)
        .astype(jnp.bfloat16)
        .reshape(tile_rows * tile_cols, hidden_dim)
    )
    grad_first = contract_rows(flat_input, err_first)
    grad_first, grad_grouped, grad_third = lax.psum(
        (grad_first, grad_grouped, grad_third), ("row", "col")
    )
    grad_input = (
        (back_third + contract_cols(err_first, first_weight))
        .astype(jnp.bfloat16)
        .reshape(tile_rows, tile_cols, in_chans)
    )
    norm_factor = 1.0 / math.sqrt(
        tile_rows * tile_cols * lax.axis_size("row") * lax.axis_size("col")
    )
    return (
        grad_input,
        grad_first * norm_factor,
        grad_grouped * norm_factor,
        grad_third * norm_factor,
    )


def solution(mesh):
    return jax.shard_map(
        body,
        mesh=mesh,
        in_specs=(
            P("row", "col", None),
            P("row", "col", None),
            P(),
            P(),
            P(),
            P(),
            P(),
            P(),
            P(),
            P(),
            P(),
        ),
        out_specs=(P("row", "col", None), P(), P(), P()),
        check_vma=False,
    )
```

profile of v0, /device:TPU:0, one launch (start us, length us, event | category | flops | bytes accessed | tf_op | source)
XLA Modules:
  0.0 193.6 jit_solution(1011616283722542725)
XLA Ops:
  7.2 1.2 fusion.28
  8.5 2.4 %collective-permute-start = (bf16[1,16,256]{2,1,0:T(8,128)(2,1)S(1)}, bf16[1,16,256]{2,1,0:T(8,128)(2,1)S(1)}, u32[]{:S(2)}, u32[]{:S(2)}) collective-permute-start(bf16[1,16,256]{2,1,0:T(8,128)(2,1)S(1)} %get-tuple-element.37), channel_id=1, source_target_pairs={{0,8},{8,16},{16,24},{1,9},{9,17},{17,25},{2,10},{10,18},{18,26},{... | collective-permute-start | bytes 24584 | tf_op jit(solution)/shard_map/ppermute | solution.py:17
  10.9 1.3 collective-permute-start.1
  12.2 0.2 select_compare_fusion
  12.4 0.9 bitcast_select_fusion
  13.2 2.8 %collective-permute-done.1 = bf16[1,16,256]{2,1,0:T(8,128)(2,1)S(1)} collective-permute-done((bf16[1,16,256]{2,1,0:T(8,128)(2,1)S(1)}, bf16[1,16,256]{2,1,0:T(8,128)(2,1)S(1)}, u32[]{:S(2)}, u32[]{:S(2)}) %collective-permute-start.1) | collective-permute-done | bytes 8224 | tf_op jit(solution)/shard_map/ppermute | solution.py:19
  16.1 3.4 %collective-permute-start.2 = (bf16[10,1,256]{2,1,0:T(2,128)(2,1)S(1)}, bf16[10,1,256]{2,1,0:T(2,128)(2,1)S(1)}, u32[]{:S(2)}, u32[]{:S(2)}) collective-permute-start(bf16[10,1,256]{2,1,0:T(2,128)(2,1)S(1)} %get-tuple-element.29), channel_id=1, source_target_pairs={{0,1},{1,2},{2,3},{3,4},{4,5},{5,6},{6,7},{8,9},{9,10},{10,11},{11... | collective-permute-start | bytes 15368 | tf_op jit(solution)/shard_map/ppermute | solution.py:17
  19.5 1.3 collective-permute-start.3
  21.0 4.1 %collective-permute-done.3 = bf16[10,1,256]{2,1,0:T(2,128)(2,1)S(1)} collective-permute-done((bf16[10,1,256]{2,1,0:T(2,128)(2,1)S(1)}, bf16[10,1,256]{2,1,0:T(2,128)(2,1)S(1)}, u32[]{:S(2)}, u32[]{:S(2)}) %collective-permute-start.3) | collective-permute-done | bytes 5152 | tf_op jit(solution)/shard_map/ppermute | solution.py:19
  25.3 0.2 convolution_add_fusion.14
  25.9 0.2 convolution_add_fusion.11
  26.1 0.2 convolution_add_fusion.10
  26.3 0.2 convolution_add_fusion.9
  26.4 0.2 fusion.29
  26.9 0.3 convert_multiply_fusion
  27.2 0.2 multiply_convert_fusion.3
  27.5 0.2 fusion.23
  27.7 0.2 fusion.24
  28.0 0.2 fusion.25
  28.2 0.2 fusion.27
  28.5 0.2 fusion.26
  28.7 0.2 fusion.22
  29.0 1.1 fusion.46
  30.0 0.3 fusion.31
  30.3 2.9 %collective-permute-start.4 = (bf16[1,16,256]{2,1,0:T(8,128)(2,1)S(1)}, bf16[1,16,256]{2,1,0:T(8,128)(2,1)S(1)}, u32[]{:S(2)}, u32[]{:S(2)}) collective-permute-start(bf16[1,16,256]{2,1,0:T(8,128)(2,1)S(1)} %get-tuple-element.33), channel_id=1, source_target_pairs={{0,8},{8,16},{16,24},{1,9},{9,17},{17,25},{2,10},{10,18},{18,26},{... | collective-permute-start | bytes 24584 | tf_op jit(solution)/shard_map/ppermute | solution.py:17
  33.2 1.3 collective-permute-start.5
  34.5 0.2 fusion.21
  34.8 0.2 fusion.20
  35.1 2.1 %collective-permute-done.5 = bf16[1,16,256]{2,1,0:T(8,128)(2,1)S(1)} collective-permute-done((bf16[1,16,256]{2,1,0:T(8,128)(2,1)S(1)}, bf16[1,16,256]{2,1,0:T(8,128)(2,1)S(1)}, u32[]{:S(2)}, u32[]{:S(2)}) %collective-permute-start.5) | collective-permute-done | bytes 8224 | tf_op jit(solution)/shard_map/ppermute | solution.py:19
  37.2 1.3 collective-permute-start.6
  38.5 5.0 %collective-permute-start.7 = (bf16[10,1,256]{2,1,0:T(2,128)(2,1)S(1)}, bf16[10,1,256]{2,1,0:T(2,128)(2,1)S(1)}, u32[]{:S(2)}, u32[]{:S(2)}) collective-permute-start(bf16[10,1,256]{2,1,0:T(2,128)(2,1)S(1)} %get-tuple-element.26), channel_id=1, source_target_pairs={{0,1},{1,2},{2,3},{3,4},{4,5},{5,6},{6,7},{8,9},{9,10},{10,11},{11... | collective-permute-start | bytes 15368 | tf_op jit(solution)/shard_map/ppermute | solution.py:17
  43.5 0.2 fusion.32
  43.8 1.1 collective-permute-done.7
  45.0 0.2 convolution_add_fusion.7
  45.2 0.2 convolution_add_fusion.6
  45.4 0.2 convolution_add_fusion.5
  45.6 0.2 convolution_add_fusion.4
  45.8 0.2 fusion.34
  46.0 0.2 convolution_add_fusion.3
  46.2 0.2 convolution_add_fusion.2
  46.5 0.2 fusion.30
  46.7 1.1 convolution_bitcast_fusion
  47.8 0.9 fusion.19
  48.7 134.5 %all-reduce.3.cloned.1.call-done = (f32[512,256]{0,1:T(8,128)}, f32[3,3,8,256]{3,2,1,0:T(8,128)}, f32[256,512]{1,0:T(8,128)}) async-done(((f32[512,256]{0,1:T(8,128)}, f32[3,3,8,256]{3,2,1,0:T(8,128)}, f32[256,512]{1,0:T(8,128)}), (f32[512,256]{0,1:T(8,128)}, f32[3,3,8,256]{3,2,1,0:T(8,128)}, f32[256,512]{1,0:T(8,128)})) %all-reduce.3.cloned.1.call-update) | async-done | bytes 1122320 | tf_op jit(solution)/shard_map/psum | solution.py:145
  183.2 1.1 broadcast_multiply_fusion.1
  184.3 1.0 copy.15
  185.3 0.6 broadcast_multiply_fusion.2
  186.0 0.8 broadcast_multiply_fusion
  (58 shorter events, 1.4 us)
Async XLA Ops:
  7.2 19.5 %copy-start = (bf16[256,512]{1,0:T(8,128)(2,1)S(1)}, bf16[256,512]{1,0:T(8,128)(2,1)}, u32[]{:S(2)}) copy-start(bf16[256,512]{1,0:T(8,128)(2,1)} %param.15) | copy-start | bytes 786436
  7.2 176.0 %all-reduce.3.cloned.1.call-start = ((), (), s32[]{:S(2)}) async-start(), calls=%async_computation | async-start | bytes 2244608 | tf_op jit(solution)/shard_map/psum | solution.py:145
  8.5 4.7 %collective-permute-start = (bf16[1,16,256]{2,1,0:T(8,128)(2,1)S(1)}, bf16[1,16,256]{2,1,0:T(8,128)(2,1)S(1)}, u32[]{:S(2)}, u32[]{:S(2)}) collective-permute-start(bf16[1,16,256]{2,1,0:T(8,128)(2,1)S(1)} %get-tuple-element.37), channel_id=1, source_target_pairs={{0,8},{8,16},{16,24},{1,9},{9,17},{17,25},{2,10},{10,18},{18,26},{... | collective-permute-start | bytes 24584 | tf_op jit(solution)/shard_map/ppermute | solution.py:17
  10.9 5.2 %collective-permute-start.1 = (bf16[1,16,256]{2,1,0:T(8,128)(2,1)S(1)}, bf16[1,16,256]{2,1,0:T(8,128)(2,1)S(1)}, u32[]{:S(2)}, u32[]{:S(2)}) collective-permute-start(bf16[1,16,256]{2,1,0:T(8,128)(2,1)S(1)} %get-tuple-element.38), channel_id=1, source_target_pairs={{8,0},{16,8},{24,16},{9,1},{17,9},{25,17},{10,2},{18,10},{26,18},{... | collective-permute-start | bytes 24584 | tf_op jit(solution)/shard_map/ppermute | solution.py:19
  16.1 4.9 %collective-permute-start.2 = (bf16[10,1,256]{2,1,0:T(2,128)(2,1)S(1)}, bf16[10,1,256]{2,1,0:T(2,128)(2,1)S(1)}, u32[]{:S(2)}, u32[]{:S(2)}) collective-permute-start(bf16[10,1,256]{2,1,0:T(2,128)(2,1)S(1)} %get-tuple-element.29), channel_id=1, source_target_pairs={{0,1},{1,2},{2,3},{3,4},{4,5},{5,6},{6,7},{8,9},{9,10},{10,11},{11... | collective-permute-start | bytes 15368 | tf_op jit(solution)/shard_map/ppermute | solution.py:17
  19.5 5.6 %collective-permute-start.3 = (bf16[10,1,256]{2,1,0:T(2,128)(2,1)S(1)}, bf16[10,1,256]{2,1,0:T(2,128)(2,1)S(1)}, u32[]{:S(2)}, u32[]{:S(2)}) collective-permute-start(bf16[10,1,256]{2,1,0:T(2,128)(2,1)S(1)} %get-tuple-element.30), channel_id=1, source_target_pairs={{1,0},{2,1},{3,2},{4,3},{5,4},{6,5},{7,6},{9,8},{10,9},{11,10},{12... | collective-permute-start | bytes 15368 | tf_op jit(solution)/shard_map/ppermute | solution.py:19
  25.8 0.9 copy-start.3
  25.9 0.9 copy-start.6
  25.9 0.9 copy-start.7
  25.9 0.9 copy-start.8
  25.9 1.0 copy-start.10
  25.9 1.0 copy-start.11
  30.3 4.8 %collective-permute-start.4 = (bf16[1,16,256]{2,1,0:T(8,128)(2,1)S(1)}, bf16[1,16,256]{2,1,0:T(8,128)(2,1)S(1)}, u32[]{:S(2)}, u32[]{:S(2)}) collective-permute-start(bf16[1,16,256]{2,1,0:T(8,128)(2,1)S(1)} %get-tuple-element.33), channel_id=1, source_target_pairs={{0,8},{8,16},{16,24},{1,9},{9,17},{17,25},{2,10},{10,18},{18,26},{... | collective-permute-start | bytes 24584 | tf_op jit(solution)/shard_map/ppermute | solution.py:17
  33.2 4.0 %collective-permute-start.5 = (bf16[1,16,256]{2,1,0:T(8,128)(2,1)S(1)}, bf16[1,16,256]{2,1,0:T(8,128)(2,1)S(1)}, u32[]{:S(2)}, u32[]{:S(2)}) collective-permute-start(bf16[1,16,256]{2,1,0:T(8,128)(2,1)S(1)} %get-tuple-element.34), channel_id=1, source_target_pairs={{8,0},{16,8},{24,16},{9,1},{17,9},{25,17},{10,2},{18,10},{26,18},{... | collective-permute-start | bytes 24584 | tf_op jit(solution)/shard_map/ppermute | solution.py:19
  35.0 10.4 %copy-start.4 = (f32[9,8,256]{2,1,0:T(8,128)}, f32[9,8,256]{2,1,0:T(8,128)S(1)}, u32[]{:S(2)}) copy-start(f32[9,8,256]{2,1,0:T(8,128)S(1)} %constant_dynamic-update-slice_fusion) | copy-start | bytes 221188
  37.2 6.5 %collective-permute-start.6 = (bf16[10,1,256]{2,1,0:T(2,128)(2,1)S(1)}, bf16[10,1,256]{2,1,0:T(2,128)(2,1)S(1)}, u32[]{:S(2)}, u32[]{:S(2)}) collective-permute-start(bf16[10,1,256]{2,1,0:T(2,128)(2,1)S(1)} %get-tuple-element.25), channel_id=1, source_target_pairs={{1,0},{2,1},{3,2},{4,3},{5,4},{6,5},{7,6},{9,8},{10,9},{11,10},{12... | collective-permute-start | bytes 15368 | tf_op jit(solution)/shard_map/ppermute | solution.py:19
  38.5 6.4 %collective-permute-start.7 = (bf16[10,1,256]{2,1,0:T(2,128)(2,1)S(1)}, bf16[10,1,256]{2,1,0:T(2,128)(2,1)S(1)}, u32[]{:S(2)}, u32[]{:S(2)}) collective-permute-start(bf16[10,1,256]{2,1,0:T(2,128)(2,1)S(1)} %get-tuple-element.26), channel_id=1, source_target_pairs={{0,1},{1,2},{2,3},{3,4},{4,5},{5,6},{6,7},{8,9},{9,10},{10,11},{11... | collective-permute-start | bytes 15368 | tf_op jit(solution)/shard_map/ppermute | solution.py:17
  45.6 1.0 copy-start.9
  46.7 1.1 copy-start.2
  183.2 2.1 %copy-start.5 = (f32[3,3,8,256]{3,2,1,0:T(8,128)S(1)}, f32[3,3,8,256]{3,2,1,0:T(8,128)}, u32[]{:S(2)}) copy-start(f32[3,3,8,256]{3,2,1,0:T(8,128)} %get-tuple-element.9) | copy-start | bytes 221188
  183.2 2.8 %copy-start.1 = (f32[256,512]{1,0:T(8,128)S(1)}, f32[256,512]{1,0:T(8,128)}, u32[]{:S(2)}) copy-start(f32[256,512]{1,0:T(8,128)} %get-tuple-element.10) | copy-start | bytes 1572868
Sparse Core Ops, SparseCore 0:
  47.9 135.2 all-reduce.2
where the time goes:
time: 194 us
  waiting for transfers between devices  145 us (75%)
  starting transfers between devices  18.8 us (10%)
  between operations  14.6 us (8%)
  matrix products  10.2 us (5%)
  other arithmetic  3.94 us (2%)
    psum x1, waiting for transfers between devices, body(): lax.psum((grad_first, grad_grouped, grad_third), ('row', 'col'))  134 us
    ppermute x4, starting transfers between devices, padded_2(): lax.ppermute(tail, axis, [(i, (i + 1) % count) for i in range(ends)])  13.6 us
    ppermute x4, waiting for transfers between devices, padded_2(): lax.ppermute(head, axis, [((i + 1) % count, i) for i in range(ends)])  9.04 us
    ppermute x4, starting transfers between devices, padded_2(): lax.ppermute(head, axis, [((i + 1) % count, i) for i in range(ends)])  5.17 us
    dot_general x11, matrix products, contract_rows(): lax.dot_general(left, right, (((0,), (0,)), ((), ())), preferred_element_...  4.27 us
  transfers between devices with their start and end apart: 9, of which 5 were waited for; matrix products, arithmetic and copies ran while one was open for 1% of the time, Pallas kernels for 0%

commit v1 on v0

v1 whole, which is shorter than its diff:
```python
import functools
import math

import jax
import jax.numpy as jnp
from jax import lax
from jax.experimental import pallas as pl
from jax.experimental.pallas import tpu as pltpu
from jax.sharding import PartitionSpec as P

MESH = pl.DeviceIdType.MESH
F32 = jnp.float32
BF16 = jnp.bfloat16
DIRS = [(dr, dc) for dr in (-1, 0, 1) for dc in (-1, 0, 1) if (dr, dc) != (0, 0)]
SLOT = {d: s for s, d in enumerate(DIRS)}
MSG = 16


def mm(left, right, lhs_dim=1, rhs_dim=0):
    return lax.dot_general(
        left, right, (((lhs_dim,), (rhs_dim,)), ((), ())), preferred_element_type=F32
    )


def remote(src, dst, send, recv, target):
    copy = pltpu.make_async_remote_copy(
        src_ref=src, dst_ref=dst, send_sem=send, recv_sem=recv, device_id=target, device_id_type=MESH
    )
    copy.start()
    return copy


def placement(th, tw, row, rows, col, cols):
    base = th * tw
    at = {d: base + MSG * s for d, s in SLOT.items()}
    cells = (th + 2) * tw
    index = lax.broadcasted_iota(jnp.int32, (cells, 1), 0)
    r = index // tw - 1
    c = index % tw
    far = 1 << 16
    no_up = (row == 0).astype(jnp.int32) * far
    no_down = (row == rows - 1).astype(jnp.int32) * far
    no_left = (col == 0).astype(jnp.int32) * far
    no_right = (col == cols - 1).astype(jnp.int32) * far
    up, down = r < 0, r >= th
    lanes = lax.broadcasted_iota(jnp.int32, (cells, base + 8 * MSG), 1)
    result = []
    for shift in (-1, 0, 1):
        cc = c + shift
        src = jnp.where(
            up, at[(-1, 0)] + cc - no_up, jnp.where(down, at[(1, 0)] + cc - no_down, r * tw + cc)
        )
        if shift == -1:
            edge = jnp.where(
                up,
                at[(-1, -1)] + tw - 1 - no_up,
                jnp.where(down, at[(1, -1)] + tw - 1 - no_down, at[(0, -1)] + th + r),
            )
            src = jnp.where(cc < 0, edge - no_left, src)
        if shift == 1:
            edge = jnp.where(
                up, at[(-1, 1)] - no_up, jnp.where(down, at[(1, 1)] - no_down, at[(0, 1)] + r)
            )
            src = jnp.where(cc >= tw, edge - no_right, src)
        result.append(jnp.where(src == lanes, 1.0, 0.0).astype(BF16))
    return result


def kernel(
    rows,
    cols,
    th,
    tw,
    x_ref,
    cot_ref,
    w1_ref,
    gw_ref,
    w3_ref,
    s1_ref,
    b1_ref,
    s2_ref,
    b2_ref,
    s3_ref,
    b3_ref,
    gin_ref,
    g1_ref,
    gk_ref,
    g3_ref,
    cells1,
    cells2,
    side1,
    side2,
    place,
    dense,
    padded1,
    padded2,
    slope1,
    slope2,
    back3,
    kgrad,
    t_part,
    t_rs,
    t_z,
    t_full,
    f_part,
    f_rs,
    f_z,
    f_full,
    halo_send,
    halo_recv,
    rs_send,
    rs_recv,
    z_send,
    z_recv,
    ag_send,
    ag_recv,
):
    row, col = lax.axis_index("row"), lax.axis_index("col")
    x, z = col % 2, col // 2
    depth = cols // 2
    plane_n = rows * 2
    me = row * 2 + x
    n = th * tw
    hid = w1_ref.shape[1]
    width = gw_ref.shape[0] // 9

    halo_peers = [
        (lax.rem(row + dr + rows, rows), lax.rem(col + dc + cols, cols)) for dr, dc in DIRS
    ]
    plane_peers = []
    for dr in range(rows):
        for dx in range(2):
            if dr or dx:
                plane_peers.append((lax.rem(row + dr, rows), z * 2 + lax.rem(x + dx, 2)))
    z_peers = [(row, lax.rem(z + dz, depth) * 2 + x) for dz in range(1, depth)]

    barrier = pltpu.get_barrier_semaphore()
    everyone = halo_peers + plane_peers + z_peers
    for peer in everyone:
        pl.semaphore_signal(barrier, inc=1, device_id=peer, device_id_type=MESH)

    def exchange(which, cells, side):
        copies = []
        for (dr, dc), peer in zip(DIRS, halo_peers):
            src = side
            if dr == -1:
                src = cells.at[pl.ds(0, tw)]
            elif dr == 1:
                src = cells.at[pl.ds(n - tw, tw)]
            there = SLOT[(-dr, -dc)]
            copies.append(
                remote(
                    src,
                    cells.at[pl.ds(n + there * MSG, MSG)],
                    halo_send.at[which, there],
                    halo_recv.at[which, there],
                    peer,
                )
            )
        return copies

    def scatter(which, part, slots):
        piece = slots.shape[1]
        copies = []
        for k, peer in enumerate(plane_peers):
            theirs = peer[0] * 2 + peer[1] % 2
            copies.append(
                remote(
                    part.at[pl.ds(pl.multiple_of(theirs * piece, 16), piece)],
                    slots.at[k],
                    rs_send.at[which, k],
                    rs_recv.at[which, k],
                    peer,
                )
            )
        return copies

    def sum_plane(copies, part, slots, total):
        piece = slots.shape[1]
        for copy in copies:
            copy.wait_recv()
        value = part[pl.ds(pl.multiple_of(me * piece, 16), piece), :].astype(F32)
        for k in range(plane_n - 1):
            value = value + slots[k].astype(F32)
        total[z] = value.astype(BF16)

    def spread(which, total):
        return [
            remote(
                total.at[z], total.at[z], z_send.at[which, k], z_recv.at[which, k], peer
            )
            for k, peer in enumerate(z_peers)
        ]

    def sum_depth(copies, total, full):
        piece = total.shape[1]
        for copy in copies:
            copy.wait_recv()
        value = total[0].astype(F32)
        for k in range(1, depth):
            value = value + total[k].astype(F32)
        full[pl.ds(pl.multiple_of(me * piece, 16), piece), :] = value.astype(BF16)

    def gather(which, total, full):
        piece = total.shape[1]
        mine = full.at[pl.ds(pl.multiple_of(me * piece, 16), piece)]
        return [
            remote(mine, mine, ag_send.at[which, k], ag_recv.at[which, k], peer)
            for k, peer in enumerate(plane_peers)
        ]

    pick_row = lax.broadcasted_iota(jnp.int32, (MSG, n), 0)
    pick_cell = lax.broadcasted_iota(jnp.int32, (MSG, n), 1)
    target = jnp.where(pick_row < th, pick_row * tw, (pick_row - th) * tw + tw - 1)
    pick = jnp.where(target == pick_cell, 1.0, 0.0).astype(BF16)

    pre1 = mm(x_ref[...], w1_ref[...]) * s1_ref[...] + b1_ref[...]
    sig = jax.nn.sigmoid(pre1)
    act1 = (pre1 * sig).astype(BF16)
    cells1[0:n, :] = act1
    side1[...] = mm(pick, act1).astype(BF16)
    pl.semaphore_wait(barrier, len(everyone))
    halo1 = exchange(0, cells1, side1)

    slope1[...] = sig * (1.0 + pre1 * (1.0 - sig)) * s1_ref[...]
    for b, matrix in enumerate(placement(th, tw, row, rows, col, cols)):
        place[b] = matrix
    same = (
        lax.broadcasted_iota(jnp.int32, (hid, hid), 0) // width
        == lax.broadcasted_iota(jnp.int32, (hid, hid), 1) // width
    )
    keep = jnp.where(same, 1.0, 0.0)
    grouped = gw_ref[...].astype(F32)
    for tap in range(9):
        small = grouped[tap * width : (tap + 1) * width]
        tiled = jnp.broadcast_to(small[None], (hid // width, width, hid)).reshape(hid, hid)
        dense[tap] = (tiled * keep).astype(BF16)
    kgrad[...] = jnp.zeros_like(kgrad)

    for copy in halo1:
        copy.wait_recv()
    for b in range(3):
        padded1[b] = mm(place[b], cells1[...]).astype(BF16)

    total = None
    for a in range(3):
        for b in range(3):
            term = mm(padded1[b, a * tw : a * tw + n, :], dense[a * 3 + b])
            total = term if total is None else total + term
    pre2 = total * s2_ref[...] + b2_ref[...]
    sig = jax.nn.sigmoid(pre2)
    act2 = (pre2 * sig).astype(BF16)
    slope2[...] = sig * (1.0 + pre2 * (1.0 - sig)) * s2_ref[...]

    pre3 = mm(act2, w3_ref[...]) * s3_ref[...] + b3_ref[...] + x_ref[...].astype(F32)
    sig = jax.nn.sigmoid(pre3)
    back = cot_ref[...].astype(F32) * (sig * (1.0 + pre3 * (1.0 - sig)))
    back3[...] = back
    err3 = (back * s3_ref[...]).astype(BF16)

    err2 = (mm(err3, w3_ref[...], 1, 1) * slope2[...]).astype(BF16)
    cells2[0:n, :] = err2
    side2[...] = mm(pick, err2).astype(BF16)
    halo2 = exchange(1, cells2, side2)

    third = mm(act2, err3, 0, 0)
    for half in range(third.shape[1] // hid):
        t_part[half * hid : (half + 1) * hid, :] = third[:, half * hid : (half + 1) * hid].astype(
            BF16
        )
    t_scatter = scatter(0, t_part, t_rs)
    for a in range(3):
        for b in range(3):
            tap = a * 3 + b
            square = mm(padded1[b, a * tw : a * tw + n, :], cells2[0:n, :], 0, 0) * keep
            kgrad[tap * width : (tap + 1) * width, :] = jnp.sum(
                square.reshape(hid // width, width, hid), axis=0
            )
    f_piece = f_rs.shape[1]
    k_piece = kgrad.shape[0] // plane_n
    w_piece = f_piece - k_piece
    for p in range(plane_n):
        f_part[p * f_piece + w_piece : (p + 1) * f_piece, :] = kgrad[
            p * k_piece : (p + 1) * k_piece, :
        ].astype(BF16)

    for copy in halo2:
        copy.wait_recv()
    for b in range(3):
        padded2[b] = mm(place[b], cells2[...]).astype(BF16)
    total = None
    for a in range(3):
        for b in range(3):
            window = padded2[2 - b, (2 - a) * tw : (2 - a) * tw + n, :]
            term = mm(window, dense[a * 3 + b], 1, 1)
            total = term if total is None else total + term
    err1 = (total * slope1[...]).astype(BF16)
    first = mm(x_ref[...], err1, 0, 0)
    for p in range(plane_n):
        f_part[p * f_piece : p * f_piece + w_piece, :] = first[
            p * w_piece : (p + 1) * w_piece
        ].astype(BF16)
    f_scatter = scatter(1, f_part, f_rs)

    sum_plane(t_scatter, t_part, t_rs, t_z)
    t_spread = spread(0, t_z)
    gin_ref[...] = (back3[...] + mm(err1, w1_ref[...], 1, 1)).astype(BF16)

    sum_plane(f_scatter, f_part, f_rs, f_z)
    f_spread = spread(1, f_z)
    sum_depth(t_spread, t_z, t_full)
    t_gather = gather(0, t_z, t_full)
    sum_depth(f_spread, f_z, f_full)
    f_gather = gather(1, f_z, f_full)

    for copy in t_gather:
        copy.wait_recv()
    for half in range(g3_ref.shape[1] // hid):
        g3_ref[:, half * hid : (half + 1) * hid] = t_full[half * hid : (half + 1) * hid, :]
    for copy in f_gather:
        copy.wait_recv()
    for p in range(plane_n):
        g1_ref[p * w_piece : (p + 1) * w_piece, :] = f_full[
            p * f_piece : p * f_piece + w_piece, :
        ]
        gk_ref[p * k_piece : (p + 1) * k_piece, :] = f_full[
            p * f_piece + w_piece : (p + 1) * f_piece, :
        ]
    for copy in halo1 + halo2 + t_scatter + f_scatter + t_spread + f_spread + t_gather + f_gather:
        copy.wait_send()


def body(mesh_rows, mesh_cols, inputs, cotangent, w1, gw, w3, s1, b1, s2, b2, s3, b3):
    th, tw, cin = inputs.shape
    hid = w1.shape[1]
    n = th * tw
    width = gw.shape[2]
    plane_n = mesh_rows * 2
    depth = mesh_cols // 2
    w_piece = cin // plane_n
    k_piece = -(-9 * width // plane_n)
    k_piece = -(-k_piece // 16) * 16
    f_piece = w_piece + k_piece
    vmem = pl.BlockSpec(memory_space=pltpu.VMEM)
    out_shape = (
        jax.ShapeDtypeStruct((n, cin), BF16),
        jax.ShapeDtypeStruct((cin, hid), BF16),
        jax.ShapeDtypeStruct((k_piece * plane_n, hid), BF16),
        jax.ShapeDtypeStruct((hid, cin), BF16),
    )
    cells = n + 8 * MSG
    padded = (3, (th + 2) * tw, hid)
    dma = pltpu.SemaphoreType.DMA
    gin, g1, gk, g3 = pl.pallas_call(
        functools.partial(kernel, mesh_rows, mesh_cols, th, tw),
        out_shape=out_shape,
        in_specs=[vmem] * 11,
        out_specs=(vmem,) * 4,
        scratch_shapes=[
            pltpu.VMEM((cells, hid), BF16),
            pltpu.VMEM((cells, hid), BF16),
            pltpu.VMEM((MSG, hid), BF16),
            pltpu.VMEM((MSG, hid), BF16),
            pltpu.VMEM((3, (th + 2) * tw, cells), BF16),
            pltpu.VMEM((9, hid, hid), BF16),
            pltpu.VMEM(padded, BF16),
            pltpu.VMEM(padded, BF16),
            pltpu.VMEM((n, hid), F32),
            pltpu.VMEM((n, hid), F32),
            pltpu.VMEM((n, cin), F32),
            pltpu.VMEM((k_piece * plane_n, hid), F32),
            pltpu.VMEM((cin, hid), BF16),
            pltpu.VMEM((plane_n - 1, w_piece, hid), BF16),
            pltpu.VMEM((depth, w_piece, hid), BF16),
            pltpu.VMEM((cin, hid), BF16),
            pltpu.VMEM((plane_n * f_piece, hid), BF16),
            pltpu.VMEM((plane_n - 1, f_piece, hid), BF16),
            pltpu.VMEM((depth, f_piece, hid), BF16),
            pltpu.VMEM((plane_n * f_piece, hid), BF16),
            dma((2, 8)),
            dma((2, 8)),
            dma((2, plane_n - 1)),
            dma((2, plane_n - 1)),
            dma((2, depth - 1)),
            dma((2, depth - 1)),
            dma((2, plane_n - 1)),
            dma((2, plane_n - 1)),
        ],
        compiler_params=pltpu.CompilerParams(
            collective_id=0, has_side_effects=True, vmem_limit_bytes=40 << 20
        ),
    )(
        inputs.reshape(n, cin),
        cotangent.reshape(n, cin),
        w1,
        gw.reshape(9 * width, hid),
        w3,
        s1.reshape(1, -1),
        b1.reshape(1, -1),
        s2.reshape(1, -1),
        b2.reshape(1, -1),
        s3.reshape(1, -1),
        b3.reshape(1, -1),
    )
    norm = 1.0 / math.sqrt(n * mesh_rows * mesh_cols)
    return (
        gin.reshape(th, tw, cin),
        g1.astype(F32) * norm,
        (gk[: 9 * width].astype(F32) * norm).reshape(gw.shape),
        g3.astype(F32) * norm,
    )


def solution(mesh):
    tile = P("row", "col", None)
    return jax.shard_map(
        functools.partial(body, mesh.shape["row"], mesh.shape["col"]),
        mesh=mesh,
        in_specs=(tile, tile) + (P(),) * 9,
        out_specs=(tile, P(), P(), P()),
        check_vma=False,
    )
```

time: 194 us -> 41.8 us (0.22)
  waiting for transfers between devices: 145 us -> 0 us
  Pallas kernels: 0 us -> 32.6 us
  starting transfers between devices: 18.8 us -> 0 us
  between operations: 14.6 us -> 0.7 us
  matrix products: 10.2 us -> 0 us
  local copies, waits for them, and re-layouts: 1.42 us -> 5.84 us
    psum x1 -> x0, waiting for transfers between devices: 134 us -> none  [body(): lax.psum((grad_first, grad_grouped, grad_third), ('row', 'col'))]
    pallas_call x0 -> x1, Pallas kernels: none -> 32.6 us  [body(): pl.pallas_call(functools.partial(kernel, mesh_rows, mesh_cols, th, tw), o...]
    ppermute x8 -> x0, starting transfers between devices: 18.8 us -> none  [the longest x4 13.6 us: padded_2(): lax.ppermute(tail, axis, [(i, (i + 1) % count) for i in range(ends)])]
    ppermute x8 -> x0, waiting for transfers between devices: 10.2 us -> none  [the longest x4 9.04 us: padded_2(): lax.ppermute(head, axis, [((i + 1) % count, i) for i in range(ends)])]
    dot_general x33 -> x0, matrix products: 10.2 us -> none  [the longest x11 4.27 us: contract_rows(): lax.dot_general(left, right, (((0,), (0,)), ((), ())), preferred_element_...]
    unnamed x33 -> x23, local copies, waits for them, and re-layouts: 1.33 us -> 5.84 us
  transfers between devices with their start and end apart: 9 -> 0, of which waited for: 5 -> 0; matrix products, arithmetic and copies ran while one was open for 1% -> 0% of each run, Pallas kernels for 0% -> 0%
where the time goes in v1:
time: 41.8 us; the launch traced here: 41.4 us
  Pallas kernels  32.6 us (78%)
  local copies, waits for them, and re-layouts  5.84 us (14%)
  other arithmetic  2.33 us (6%)
  between operations  0.7 us (2%)
    pallas_call x1, Pallas kernels, body(): pl.pallas_call(functools.partial(kernel, mesh_rows, mesh_cols, th, tw), o...  32.6 us
    unnamed x23, local copies, waits for them, and re-layouts  5.84 us
    mul x1, other arithmetic, body(): g3.astype(F32) * norm  0.86 us

profile of v1, /device:TPU:0, one launch (start us, length us, event | category | flops | bytes accessed | tf_op | source)
XLA Modules:
  0.0 41.4 jit_solution(12584490324916558608)
XLA Ops:
  0.6 0.0 copy-start.10
  0.6 0.0 copy-start.8
  0.7 0.0 copy-start.9
  0.7 0.0 copy-start.6
  0.7 0.0 copy-start.5
  0.7 0.0 copy-start.7
  0.7 0.6 %copy-done.10 = f32[256]{0:T(256)S(1)} copy-done((f32[256]{0:T(256)S(1)}, f32[256]{0:T(256)}, u32[]{:S(2)}) %copy-start.10) | copy-done | bytes 1048
  1.3 0.0 copy-done.8
  1.3 0.0 copy-done.9
  1.3 0.0 copy-done.6
  1.4 0.0 copy-done.5
  1.4 0.0 copy-done.7
  1.4 0.0 copy-start
  1.4 0.9 %copy-done = bf16[512,256]{1,0:T(8,128)(2,1)S(1)} copy-done((bf16[512,256]{1,0:T(8,128)(2,1)S(1)}, bf16[512,256]{1,0:T(8,128)(2,1)}, u32[]{:S(2)}) %copy-start) | copy-done | bytes 262168
  2.3 0.0 copy-start.1
  2.3 0.9 %copy-done.1 = bf16[256,512]{1,0:T(8,128)(2,1)S(1)} copy-done((bf16[256,512]{1,0:T(8,128)(2,1)S(1)}, bf16[256,512]{1,0:T(8,128)(2,1)}, u32[]{:S(2)}) %copy-start.1) | copy-done | bytes 262168
  3.3 0.0 copy-start.2
  3.3 0.9 %copy-done.2 = bf16[8,16,512]{2,1,0:T(8,128)(2,1)S(1)} copy-done((bf16[8,16,512]{2,1,0:T(8,128)(2,1)S(1)}, bf16[8,16,512]{2,1,0:T(8,128)(2,1)}, u32[]{:S(2)}) %copy-start.2) | copy-done | bytes 131096
  4.2 0.0 copy-start.3
  4.2 0.9 %copy-done.3 = bf16[8,16,512]{2,1,0:T(8,128)(2,1)S(1)} copy-done((bf16[8,16,512]{2,1,0:T(8,128)(2,1)S(1)}, bf16[8,16,512]{2,1,0:T(8,128)(2,1)}, u32[]{:S(2)}) %copy-start.3) | copy-done | bytes 131096
  5.1 0.0 copy-start.4
  5.1 0.8 %copy-done.4 = bf16[3,3,8,256]{3,2,1,0:T(8,128)(2,1)S(1)} copy-done((bf16[3,3,8,256]{3,2,1,0:T(8,128)(2,1)S(1)}, bf16[3,3,8,256]{3,2,1,0:T(8,128)(2,1)}, u32[]{:S(2)}) %copy-start.4) | copy-done | bytes 36888
  5.9 32.6 %shard_map.138 = (bf16[128,512]{1,0:T(8,128)(2,1)S(1)}, bf16[512,256]{1,0:T(8,128)(2,1)S(1)}, bf16[128,256]{1,0:T(8,128)(2,1)S(1)}, bf16[256,512]{1,0:T(8,128)(2,1)S(1)}) custom-call(bf16[128,512]{1,0:T(8,128)(2,1)S(1)} %bitcast.11, bf16[128,512]{1,0:T(8,128)(2,1)S(1)} %bitcast.12, bf16[512,256]{1,0:T(8,128)(2,1)S(1)} %copy-done, ...), custom_call_target="tpu_custom_call" | custom-call | tf_op jit(solution)/shard_map/pallas_call | solution.py:354
  38.5 0.9 %convert_multiply_fusion = f32[256,512]{1,0:T(8,128)} fusion(bf16[256,512]{1,0:T(8,128)(2,1)S(1)} %get-tuple-element.11), kind=kLoop, calls=%fused_computation | loop fusion | flops 262144 | bytes 786432 | tf_op jit(solution)/shard_map/mul | solution.py:410
  39.3 0.8 %convert_multiply_fusion.1 = f32[512,256]{1,0:T(8,128)} fusion(bf16[512,256]{1,0:T(8,128)(2,1)S(1)} %get-tuple-element.9), kind=kLoop, calls=%fused_computation.1 | loop fusion | flops 262144 | bytes 786432 | tf_op jit(solution)/shard_map/mul | solution.py:408
  40.2 0.6 %convert_multiply_fusion.2 = f32[72,256]{1,0:T(8,128)} fusion(bf16[128,256]{1,0:T(8,128)(2,1)S(1)} %get-tuple-element.10), kind=kLoop, calls=%fused_computation.2 | loop fusion | flops 36864 | bytes 110592 | tf_op jit(solution)/shard_map/mul | solution.py:409
  40.8 0.7 %copy.16 = bf16[8,16,512]{2,1,0:T(8,128)(2,1)} copy(bf16[8,16,512]{2,1,0:T(8,128)(2,1)S(1)} %bitcast.13) | data formatting | bytes 262144
Async XLA Ops:
  0.6 0.7 %copy-start.10 = (f32[256]{0:T(256)S(1)}, f32[256]{0:T(256)}, u32[]{:S(2)}) copy-start(f32[256]{0:T(256)} %param.19) | copy-start | bytes 3076
  0.6 0.7 %copy-start.8 = (f32[256]{0:T(256)S(1)}, f32[256]{0:T(256)}, u32[]{:S(2)}) copy-start(f32[256]{0:T(256)} %param.17) | copy-start | bytes 3076
  0.7 0.7 %copy-start.9 = (f32[256]{0:T(256)S(1)}, f32[256]{0:T(256)}, u32[]{:S(2)}) copy-start(f32[256]{0:T(256)} %param.18) | copy-start | bytes 3076
  0.7 0.7 %copy-start.6 = (f32[512]{0:T(512)S(1)}, f32[512]{0:T(512)}, u32[]{:S(2)}) copy-start(f32[512]{0:T(512)} %param.21) | copy-start | bytes 6148
  0.7 0.7 %copy-start.5 = (f32[512]{0:T(512)S(1)}, f32[512]{0:T(512)}, u32[]{:S(2)}) copy-start(f32[512]{0:T(512)} %param.20) | copy-start | bytes 6148
  0.7 0.7 %copy-start.7 = (f32[256]{0:T(256)S(1)}, f32[256]{0:T(256)}, u32[]{:S(2)}) copy-start(f32[256]{0:T(256)} %param.16) | copy-start | bytes 3076
  1.4 0.9 %copy-start = (bf16[512,256]{1,0:T(8,128)(2,1)S(1)}, bf16[512,256]{1,0:T(8,128)(2,1)}, u32[]{:S(2)}) copy-start(bf16[512,256]{1,0:T(8,128)(2,1)} %w1_ref.1) | copy-start | bytes 786436
  2.3 0.9 %copy-start.1 = (bf16[256,512]{1,0:T(8,128)(2,1)S(1)}, bf16[256,512]{1,0:T(8,128)(2,1)}, u32[]{:S(2)}) copy-start(bf16[256,512]{1,0:T(8,128)(2,1)} %w3_ref.1) | copy-start | bytes 786436
  3.3 0.9 %copy-start.2 = (bf16[8,16,512]{2,1,0:T(8,128)(2,1)S(1)}, bf16[8,16,512]{2,1,0:T(8,128)(2,1)}, u32[]{:S(2)}) copy-start(bf16[8,16,512]{2,1,0:T(8,128)(2,1)} %param.11) | copy-start | bytes 393220
  4.2 0.9 %copy-start.3 = (bf16[8,16,512]{2,1,0:T(8,128)(2,1)S(1)}, bf16[8,16,512]{2,1,0:T(8,128)(2,1)}, u32[]{:S(2)}) copy-start(bf16[8,16,512]{2,1,0:T(8,128)(2,1)} %param.12) | copy-start | bytes 393220
  5.1 0.8 %copy-start.4 = (bf16[3,3,8,256]{3,2,1,0:T(8,128)(2,1)S(1)}, bf16[3,3,8,256]{3,2,1,0:T(8,128)(2,1)}, u32[]{:S(2)}) copy-start(bf16[3,3,8,256]{3,2,1,0:T(8,128)(2,1)} %param.14) | copy-start | bytes 110596

commit v2 on v1

--- a/solution.py
+++ b/solution.py
@@ -14,6 +14,8 @@
 DIRS = [(dr, dc) for dr in (-1, 0, 1) for dc in (-1, 0, 1) if (dr, dc) != (0, 0)]
 SLOT = {d: s for s, d in enumerate(DIRS)}
 MSG = 16
+PARTS = 2
+LOAD_ORDER = (0, 2, 5, 6, 3, 7, 8, 4, 9, 10, 1)
 
 
 def mm(left, right, lhs_dim=1, rhs_dim=0):
@@ -66,55 +68,24 @@
     return result
 
 
-def kernel(
-    rows,
-    cols,
-    th,
-    tw,
-    x_ref,
-    cot_ref,
-    w1_ref,
-    gw_ref,
-    w3_ref,
-    s1_ref,
-    b1_ref,
-    s2_ref,
-    b2_ref,
-    s3_ref,
-    b3_ref,
-    gin_ref,
-    g1_ref,
-    gk_ref,
-    g3_ref,
-    cells1,
-    cells2,
-    side1,
-    side2,
-    place,
-    dense,
-    padded1,
-    padded2,
-    slope1,
-    slope2,
-    back3,
-    kgrad,
-    t_part,
-    t_rs,
-    t_z,
-    t_full,
-    f_part,
-    f_rs,
-    f_z,
-    f_full,
-    halo_send,
-    halo_recv,
-    rs_send,
-    rs_recv,
-    z_send,
-    z_recv,
-    ag_send,
-    ag_recv,
-):
+def kernel(rows, cols, th, tw, chunks, norm, *refs):
+    hbm, refs = refs[:11], refs[11:]
+    outs = refs[:4]
+    local, refs = refs[4:15], refs[15:]
+    x_ref, cot_ref, w1_ref, gw_ref, w3_ref, s1_ref, b1_ref, s2_ref, b2_ref, s3_ref, b3_ref = local
+    cells1, cells2, side1, side2, place, dense, padded1, padded2 = refs[:8]
+    slope1, slope2, back3, kgrad, x_turned = refs[8:13]
+    gin_ref, g1_ref, gk_ref, g3_ref = refs[13:17]
+    refs = refs[4:]
+    units = [refs[13 + 4 * u : 17 + 4 * u] for u in range(2 + chunks)]
+    (load_sem, out_sem, halo_send, halo_recv, rs_send, rs_recv, z_send, z_recv, ag_send, ag_recv) = refs[
+        13 + 4 * (2 + chunks) :
+    ]
+    loads = []
+    for index in LOAD_ORDER:
+        copy = pltpu.make_async_copy(hbm[index], local[index], load_sem.at[index])
+        copy.start()
+        loads.append(copy)
     row, col = lax.axis_index("row"), lax.axis_index("col")
     x, z = col % 2, col // 2
     depth = cols // 2
@@ -134,30 +105,67 @@
                 plane_peers.append((lax.rem(row + dr, rows), z * 2 + lax.rem(x + dx, 2)))
     z_peers = [(row, lax.rem(z + dz, depth) * 2 + x) for dz in range(1, depth)]
 
+    def exists(dr, dc):
+        ok = None
+        for step, spot, count in ((dr, row, rows), (dc, col, cols)):
+            if step:
+                inside = spot > 0 if step < 0 else spot < count - 1
+                ok = inside if ok is None else jnp.logical_and(ok, inside)
+        return ok
+
+    for cells in (cells1, cells2):
+        cells[n:, :] = jnp.zeros((8 * MSG, hid), BF16)
+
     barrier = pltpu.get_barrier_semaphore()
-    everyone = halo_peers + plane_peers + z_peers
-    for peer in everyone:
+    for peer in plane_peers + z_peers:
         pl.semaphore_signal(barrier, inc=1, device_id=peer, device_id_type=MESH)
+    for (dr, dc), peer in zip(DIRS, halo_peers):
+
+        @pl.when(exists(dr, dc))
+        def _(peer=peer):
+            pl.semaphore_signal(barrier, inc=1, device_id=peer, device_id_type=MESH)
+
+    near_rows = 1 + (row > 0).astype(jnp.int32) + (row < rows - 1).astype(jnp.int32)
+    near_cols = 1 + (col > 0).astype(jnp.int32) + (col < cols - 1).astype(jnp.int32)
+    greeted = near_rows * near_cols - 1 + len(plane_peers) + len(z_peers)
+
+    def border(which, cells, side, d, arriving):
+        dr, dc = d
+        src = side
+        if dr == -1:
+            src = cells.at[pl.ds(0, tw)]
+        elif dr == 1:
+            src = cells.at[pl.ds(n - tw, tw)]
+        slot = SLOT[d] if arriving else SLOT[(-dr, -dc)]
+        return pltpu.make_async_remote_copy(
+            src_ref=src,
+            dst_ref=cells.at[pl.ds(n + slot * MSG, MSG)],
+            send_sem=halo_send.at[which, slot],
+            recv_sem=halo_recv.at[which, slot],
+            device_id=halo_peers[SLOT[d]],
+            device_id_type=MESH,
+        )
 
     def exchange(which, cells, side):
-        copies = []
-        for (dr, dc), peer in zip(DIRS, halo_peers):
-            src = side
-            if dr == -1:
-                src = cells.at[pl.ds(0, tw)]
-            elif dr == 1:
-                src = cells.at[pl.ds(n - tw, tw)]
-            there = SLOT[(-dr, -dc)]
-            copies.append(
-                remote(
-                    src,
-                    cells.at[pl.ds(n + there * MSG, MSG)],
-                    halo_send.at[which, there],
-                    halo_recv.at[which, there],
-                    peer,
-                )
-            )
-        return copies
+        for d in DIRS:
+
+            @pl.when(exists(*d))
+            def _(d=d):
+                border(which, cells, side, d, False).start()
+
+    def arrive(which, cells, side):
+        for d in DIRS:
+
+            @pl.when(exists(*d))
+            def _(d=d):
+                border(which, cells, side, d, True).wait_recv()
+
+    def depart(which, cells, side):
+        for d in DIRS:
+
+            @pl.when(exists(*d))
+            def _(d=d):
+                border(which, cells, side, d, False).wait_send()
 
     def scatter(which, part, slots):
         piece = slots.shape[1]
@@ -214,13 +222,17 @@
     target = jnp.where(pick_row < th, pick_row * tw, (pick_row - th) * tw + tw - 1)
     pick = jnp.where(target == pick_cell, 1.0, 0.0).astype(BF16)
 
+    for copy in loads[:4]:
+        copy.wait()
     pre1 = mm(x_ref[...], w1_ref[...]) * s1_ref[...] + b1_ref[...]
     sig = jax.nn.sigmoid(pre1)
     act1 = (pre1 * sig).astype(BF16)
     cells1[0:n, :] = act1
     side1[...] = mm(pick, act1).astype(BF16)
-    pl.semaphore_wait(barrier, len(everyone))
-    halo1 = exchange(0, cells1, side1)
+    pl.semaphore_wait(barrier, greeted)
+    exchange(0, cells1, side1)
+    for copy in loads[4:]:
+        copy.wait()
 
     slope1[...] = sig * (1.0 + pre1 * (1.0 - sig)) * s1_ref[...]
     for b, matrix in enumerate(placement(th, tw, row, rows, col, cols)):
@@ -237,8 +249,9 @@
         dense[tap] = (tiled * keep).astype(BF16)
     kgrad[...] = jnp.zeros_like(kgrad)
 
-    for copy in halo1:
-        copy.wait_recv()
+    x_turned[...] = x_ref[...].T
+
+    arrive(0, cells1, side1)
     for b in range(3):
         padded1[b] = mm(place[b], cells1[...]).astype(BF16)
 
@@ -261,14 +274,29 @@
     err2 = (mm(err3, w3_ref[...], 1, 1) * slope2[...]).astype(BF16)
     cells2[0:n, :] = err2
     side2[...] = mm(pick, err2).astype(BF16)
-    halo2 = exchange(1, cells2, side2)
+    exchange(1, cells2, side2)
+
+    started = []
+
+    def unit(index, step, *extra):
+        part, slots, total, full = units[index]
+        if step == 0:
+            copies = scatter(index, part, slots)
+        elif step == 1:
+            sum_plane(*extra, part, slots, total)
+            copies = spread(index, total)
+        else:
+            sum_depth(*extra, total, full)
+            copies = gather(index, total, full)
+        started.extend(copies)
+        return copies
 
     third = mm(act2, err3, 0, 0)
     for half in range(third.shape[1] // hid):
-        t_part[half * hid : (half + 1) * hid, :] = third[:, half * hid : (half + 1) * hid].astype(
-            BF16
-        )
-    t_scatter = scatter(0, t_part, t_rs)
+        units[0][0][half * hid : (half + 1) * hid, :] = third[
+            :, half * hid : (half + 1) * hid
+        ].astype(BF16)
+    t_now = unit(0, 0)
     for a in range(3):
         for b in range(3):
             tap = a * 3 + b
@@ -276,16 +304,10 @@
             kgrad[tap * width : (tap + 1) * width, :] = jnp.sum(
                 square.reshape(hid // width, width, hid), axis=0
             )
-    f_piece = f_rs.shape[1]
-    k_piece = kgrad.shape[0] // plane_n
-    w_piece = f_piece - k_piece
-    for p in range(plane_n):
-        f_part[p * f_piece + w_piece : (p + 1) * f_piece, :] = kgrad[
-            p * k_piece : (p + 1) * k_piece, :
-        ].astype(BF16)
-
-    for copy in halo2:
-        copy.wait_recv()
+    units[1][0][...] = kgrad[...].astype(BF16)
+    k_now = unit(1, 0)
+
+    arrive(1, cells2, side2)
     for b in range(3):
         padded2[b] = mm(place[b], cells2[...]).astype(BF16)
     total = None
@@ -295,39 +317,73 @@
             term = mm(window, dense[a * 3 + b], 1, 1)
             total = term if total is None else total + term
     err1 = (total * slope1[...]).astype(BF16)
-    first = mm(x_ref[...], err1, 0, 0)
-    for p in range(plane_n):
-        f_part[p * f_piece : p * f_piece + w_piece, :] = first[
-            p * w_piece : (p + 1) * w_piece
-        ].astype(BF16)
-    f_scatter = scatter(1, f_part, f_rs)
-
-    sum_plane(t_scatter, t_part, t_rs, t_z)
-    t_spread = spread(0, t_z)
+    span = hid // chunks
+    f_now = []
+    for chunk in range(chunks):
+        units[2 + chunk][0][...] = mm(
+            x_turned[...], err1[:, chunk * span : (chunk + 1) * span]
+        ).astype(BF16)
+        f_now.append(unit(2 + chunk, 0))
+
+    t_now = unit(0, 1, t_now)
+    k_now = unit(1, 1, k_now)
+    for chunk in range(chunks):
+        f_now[chunk] = unit(2 + chunk, 1, f_now[chunk])
+    t_now = unit(0, 2, t_now)
+    k_now = unit(1, 2, k_now)
+    for chunk in range(chunks):
+        f_now[chunk] = unit(2 + chunk, 2, f_now[chunk])
     gin_ref[...] = (back3[...] + mm(err1, w1_ref[...], 1, 1)).astype(BF16)
-
-    sum_plane(f_scatter, f_part, f_rs, f_z)
-    f_spread = spread(1, f_z)
-    sum_depth(t_spread, t_z, t_full)
-    t_gather = gather(0, t_z, t_full)
-    sum_depth(f_spread, f_z, f_full)
-    f_gather = gather(1, f_z, f_full)
-
-    for copy in t_gather:
+    stores = []
+
+    def store(src, dst):
+        copy = pltpu.make_async_copy(src, dst, out_sem.at[len(stores)])
+        copy.start()
+        stores.append(copy)
+
+    store(gin_ref, outs[0])
+    for copy in t_now:
         copy.wait_recv()
     for half in range(g3_ref.shape[1] // hid):
-        g3_ref[:, half * hid : (half + 1) * hid] = t_full[half * hid : (half + 1) * hid, :]
-    for copy in f_gather:
+        g3_ref[:, half * hid : (half + 1) * hid] = (
+            units[0][3][half * hid : (half + 1) * hid, :].astype(F32) * norm
+        )
+    store(g3_ref, outs[3])
+    for copy in k_now:
         copy.wait_recv()
-    for p in range(plane_n):
-        g1_ref[p * w_piece : (p + 1) * w_piece, :] = f_full[
-            p * f_piece : p * f_piece + w_piece, :
-        ]
-        gk_ref[p * k_piece : (p + 1) * k_piece, :] = f_full[
-            p * f_piece + w_piece : (p + 1) * f_piece, :
-        ]
-    for copy in halo1 + halo2 + t_scatter + f_scatter + t_spread + f_spread + t_gather + f_gather:
+    gk_ref[...] = units[1][3][...].astype(F32)[: gk_ref.shape[0]] * norm
+    store(gk_ref, outs[2])
+    for chunk in range(chunks):
+        for copy in f_now[chunk]:
+            copy.wait_recv()
+        lanes = pl.ds(chunk * span, span)
+        g1_ref[:, lanes] = units[2 + chunk][3][...].astype(F32) * norm
+        store(g1_ref.at[:, lanes], outs[1].at[:, lanes])
+    depart(0, cells1, side1)
+    depart(1, cells2, side2)
+    for copy in started:
         copy.wait_send()
+    for copy in stores:
+        copy.wait()
+
+
+def finish(*refs):
+    sources, targets, held, sems = refs[:4], refs[4:8], refs[8:12], refs[12]
+    reads, writes = [], []
+    for k, (src, dst, hold) in enumerate(zip(sources, targets, held)):
+        parts = PARTS if src.shape[0] % (16 * PARTS) == 0 else 1
+        size = src.shape[0] // parts
+        for part in range(parts):
+            span = pl.ds(part * size, size)
+            reads.append(pltpu.make_async_copy(src.at[span], hold.at[span], sems.at[0, k, part]))
+            writes.append(pltpu.make_async_copy(hold.at[span], dst.at[span], sems.at[1, k, part]))
+    for copy in reads:
+        copy.start()
+    for read, write in zip(reads, writes):
+        read.wait()
+        write.start()
+    for copy in writes:
+        copy.wait()
 
 
 def body(mesh_rows, mesh_cols, inputs, cotangent, w1, gw, w3, s1, b1, s2, b2, s3, b3):
@@ -337,26 +393,52 @@
     width = gw.shape[2]
     plane_n = mesh_rows * 2
     depth = mesh_cols // 2
+    chunks = 2
     w_piece = cin // plane_n
     k_piece = -(-9 * width // plane_n)
     k_piece = -(-k_piece // 16) * 16
-    f_piece = w_piece + k_piece
-    vmem = pl.BlockSpec(memory_space=pltpu.VMEM)
+    hbm = pl.BlockSpec(memory_space=pltpu.HBM)
     out_shape = (
         jax.ShapeDtypeStruct((n, cin), BF16),
-        jax.ShapeDtypeStruct((cin, hid), BF16),
-        jax.ShapeDtypeStruct((k_piece * plane_n, hid), BF16),
-        jax.ShapeDtypeStruct((hid, cin), BF16),
+        jax.ShapeDtypeStruct((cin, hid), F32),
+        jax.ShapeDtypeStruct((9 * width, hid), F32),
+        jax.ShapeDtypeStruct((hid, cin), F32),
+    )
+    norm = 1.0 / math.sqrt(n * mesh_rows * mesh_cols)
+    operands = (
+        inputs.reshape(n, cin),
+        cotangent.reshape(n, cin),
+        w1,
+        gw.reshape(9 * width, hid),
+        w3,
+        s1.reshape(1, -1),
+        b1.reshape(1, -1),
+        s2.reshape(1, -1),
+        b2.reshape(1, -1),
+        s3.reshape(1, -1),
+        b3.reshape(1, -1),
     )
     cells = n + 8 * MSG
     padded = (3, (th + 2) * tw, hid)
     dma = pltpu.SemaphoreType.DMA
-    gin, g1, gk, g3 = pl.pallas_call(
-        functools.partial(kernel, mesh_rows, mesh_cols, th, tw),
+    unit_shapes = [(w_piece, hid), (k_piece, hid)] + [(w_piece, hid // chunks)] * chunks
+    unit_scratch = []
+    for piece, wide in unit_shapes:
+        for shape in (
+            (plane_n * piece, wide),
+            (plane_n - 1, piece, wide),
+            (depth, piece, wide),
+            (plane_n * piece, wide),
+        ):
+            unit_scratch.append(pltpu.VMEM(shape, BF16))
+    count = 2 + chunks
+    results = pl.pallas_call(
+        functools.partial(kernel, mesh_rows, mesh_cols, th, tw, chunks, norm),
         out_shape=out_shape,
-        in_specs=[vmem] * 11,
-        out_specs=(vmem,) * 4,
-        scratch_shapes=[
+        in_specs=[hbm] * 11,
+        out_specs=(hbm,) * 4,
+        scratch_shapes=[pltpu.VMEM(a.shape, a.dtype) for a in operands]
+        + [
             pltpu.VMEM((cells, hid), BF16),
             pltpu.VMEM((cells, hid), BF16),
             pltpu.VMEM((MSG, hid), BF16),
@@ -369,46 +451,35 @@
             pltpu.VMEM((n, hid), F32),
             pltpu.VMEM((n, cin), F32),
             pltpu.VMEM((k_piece * plane_n, hid), F32),
-            pltpu.VMEM((cin, hid), BF16),
-            pltpu.VMEM((plane_n - 1, w_piece, hid), BF16),
-            pltpu.VMEM((depth, w_piece, hid), BF16),
-            pltpu.VMEM((cin, hid), BF16),
-            pltpu.VMEM((plane_n * f_piece, hid), BF16),
-            pltpu.VMEM((plane_n - 1, f_piece, hid), BF16),
-            pltpu.VMEM((depth, f_piece, hid), BF16),
-            pltpu.VMEM((plane_n * f_piece, hid), BF16),
+            pltpu.VMEM((cin, n), BF16),
+        ]
+        + [pltpu.VMEM(a.shape, a.dtype) for a in out_shape]
+        + unit_scratch
+        + [
+            dma((11,)),
+            dma((3 + chunks,)),
             dma((2, 8)),
             dma((2, 8)),
-            dma((2, plane_n - 1)),
-            dma((2, plane_n - 1)),
-            dma((2, depth - 1)),
-            dma((2, depth - 1)),
-            dma((2, plane_n - 1)),
-            dma((2, plane_n - 1)),
+            dma((count, plane_n - 1)),
+            dma((count, plane_n - 1)),
+            dma((count, depth - 1)),
+            dma((count, depth - 1)),
+            dma((count, plane_n - 1)),
+            dma((count, plane_n - 1)),
         ],
         compiler_params=pltpu.CompilerParams(
-            collective_id=0, has_side_effects=True, vmem_limit_bytes=40 << 20
+            collective_id=0, has_side_effects=True, vmem_limit_bytes=60 << 20
         ),
-    )(
-        inputs.reshape(n, cin),
-        cotangent.reshape(n, cin),
-        w1,
-        gw.reshape(9 * width, hid),
-        w3,
-        s1.reshape(1, -1),
-        b1.reshape(1, -1),
-        s2.reshape(1, -1),
-        b2.reshape(1, -1),
-        s3.reshape(1, -1),
-        b3.reshape(1, -1),
-    )
-    norm = 1.0 / math.sqrt(n * mesh_rows * mesh_cols)
-    return (
-        gin.reshape(th, tw, cin),
-        g1.astype(F32) * norm,
-        (gk[: 9 * width].astype(F32) * norm).reshape(gw.shape),
-        g3.astype(F32) * norm,
-    )
+    )(*operands)
+    gin, g1, gk, g3 = pl.pallas_call(
+        finish,
+        out_shape=out_shape,
+        in_specs=[hbm] * 4,
+        out_specs=(hbm,) * 4,
+        scratch_shapes=[pltpu.VMEM(a.shape, a.dtype) for a in out_shape] + [dma((2, 4, PARTS))],
+        compiler_params=pltpu.CompilerParams(vmem_limit_bytes=60 << 20),
+    )(*results)
+    return gin.reshape(th, tw, cin), g1, gk.reshape(gw.shape), g3
 
 
 def solution(mesh):

time: 41.8 us -> 34.1 us (0.82)
  local copies, waits for them, and re-layouts: 5.84 us -> 0 us
  other arithmetic: 2.33 us -> 0 us
  Pallas kernels: 32.6 us -> 33.2 us
    unnamed x23 -> x0, local copies, waits for them, and re-layouts: 5.84 us -> none
    mul x3 -> x0, other arithmetic: 2.33 us -> none  [the longest x1 0.86 us: body(): g3.astype(F32) * norm]
    pallas_call x1 -> x2, Pallas kernels: 32.6 us -> 33.2 us  [the longest x1 31 us: body(): pl.pallas_call(functools.partial(kernel, mesh_rows, mesh_cols, th, tw, ch...]
where the time goes in v2:
time: 34.1 us; the launch traced here: 33.8 us
  Pallas kernels  33.2 us (97%)
  between operations  0.64 us (2%)
    pallas_call x1, Pallas kernels, body(): pl.pallas_call(functools.partial(kernel, mesh_rows, mesh_cols, th, tw, ch...  31 us
    pallas_call x1, Pallas kernels, body(): pl.pallas_call(finish, out_shape=out_shape, in_specs=[hbm] * 4, out_specs...  2.16 us

profile of v2, /device:TPU:0, one launch (start us, length us, event | category | flops | bytes accessed | tf_op | source)
XLA Modules:
  0.0 33.8 jit_solution(14968924876659536742)
XLA Ops:
  0.6 31.0 %shard_map.138 = (bf16[128,512]{1,0:T(8,128)(2,1)}, f32[512,256]{1,0:T(8,128)}, f32[72,256]{1,0:T(8,128)}, f32[256,512]{1,0:T(8,128)}) custom-call(bf16[128,512]{1,0:T(8,128)(2,1)} %bitcast.11, bf16[128,512]{1,0:T(8,128)(2,1)} %bitcast.12, bf16[512,256]{1,0:T(8,128)(2,1)} %refs_2_.1, bf16[72,256]{1,0:T(8,128)(2,1)} %bitcast.13, bf16[256,512]{1,0:T(8,128)(2,1)} %refs_4_.1, ...), custom_call_target="tpu_custom_call" | custom-call | tf_op jit(solution)/shard_map/pallas_call | solution.py:435
  31.7 2.2 %shard_map.139 = (bf16[128,512]{1,0:T(8,128)(2,1)}, f32[512,256]{1,0:T(8,128)}, f32[72,256]{1,0:T(8,128)}, f32[256,512]{1,0:T(8,128)}) custom-call(bf16[128,512]{1,0:T(8,128)(2,1)} %get-tuple-element.12.refs_0_, f32[512,256]{1,0:T(8,128)} %get-tuple-element.13.refs_1_, f32[72,256]{1,0:T(8,128)} %get-tuple-element.14.refs_2_, ...), custom_call_target="tpu_custom_call" | custom-call | tf_op jit(solution)/shard_map/pallas_call | solution.py:474

commit v3 on v2

--- a/solution.py
+++ b/solution.py
@@ -209,13 +209,32 @@
             value = value + total[k].astype(F32)
         full[pl.ds(pl.multiple_of(me * piece, 16), piece), :] = value.astype(BF16)
 
+    partner = (row + 1 - 2 * lax.rem(row, 2), col)
+    across = [(dr, dx) for dr in range(0, rows, 2) for dx in range(2) if dr or dx]
+
     def gather(which, total, full):
         piece = total.shape[1]
         mine = full.at[pl.ds(pl.multiple_of(me * piece, 16), piece)]
+        targets = [partner] + [
+            (lax.rem(row + dr, rows), z * 2 + lax.rem(x + dx, 2)) for dr, dx in across
+        ]
         return [
             remote(mine, mine, ag_send.at[which, k], ag_recv.at[which, k], peer)
-            for k, peer in enumerate(plane_peers)
+            for k, peer in enumerate(targets)
         ]
+
+    def relay(which, copies, full):
+        piece = full.shape[0] // plane_n
+        passed = []
+        for k, (dr, dx) in enumerate(across):
+            copies[1 + k].wait_recv()
+            origin = lax.rem(row - dr + rows, rows) * 2 + lax.rem(x + dx, 2)
+            held = full.at[pl.ds(pl.multiple_of(origin * piece, 16), piece)]
+            slot = 1 + len(across) + k
+            passed.append(
+                remote(held, held, ag_send.at[which, slot], ag_recv.at[which, slot], partner)
+            )
+        return copies[:1] + passed
 
     pick_row = lax.broadcasted_iota(jnp.int32, (MSG, n), 0)
     pick_cell = lax.broadcasted_iota(jnp.int32, (MSG, n), 1)
@@ -290,6 +309,11 @@
             copies = gather(index, total, full)
         started.extend(copies)
         return copies
+
+    def forward(index, copies):
+        result = relay(index, copies, units[index][3])
+        started.extend(result[1:])
+        return result
 
     third = mm(act2, err3, 0, 0)
     for half in range(third.shape[1] // hid):
@@ -333,6 +357,8 @@
     k_now = unit(1, 2, k_now)
     for chunk in range(chunks):
         f_now[chunk] = unit(2 + chunk, 2, f_now[chunk])
+    t_now = forward(0, t_now)
+    k_now = forward(1, k_now)
     gin_ref[...] = (back3[...] + mm(err1, w1_ref[...], 1, 1)).astype(BF16)
     stores = []
 
@@ -342,6 +368,8 @@
         stores.append(copy)
 
     store(gin_ref, outs[0])
+    for chunk in range(chunks):
+        f_now[chunk] = forward(2 + chunk, f_now[chunk])
     for copy in t_now:
         copy.wait_recv()
     for half in range(g3_ref.shape[1] // hid):

time: 34.1 us -> 33.7 us (0.988)
  Pallas kernels: 33.2 us -> 32.5 us
    pallas_call x1, Pallas kernels: 31 us -> 30.3 us  [body(): pl.pallas_call(functools.partial(kernel, mesh_rows, mesh_cols, th, tw, ch...]
where the time goes in v3:
time: 33.7 us; the launch traced here: 33.1 us
  Pallas kernels  32.5 us (96%)
  between operations  0.64 us (2%)
    pallas_call x1, Pallas kernels, body(): pl.pallas_call(functools.partial(kernel, mesh_rows, mesh_cols, th, tw, ch...  30.3 us
    pallas_call x1, Pallas kernels, body(): pl.pallas_call(finish, out_shape=out_shape, in_specs=[hbm] * 4, out_specs...  2.16 us

profile of v3, /device:TPU:0, one launch (start us, length us, event | category | flops | bytes accessed | tf_op | source)
XLA Modules:
  0.0 33.1 jit_solution(9901597666275602543)
XLA Ops:
  0.6 30.3 %shard_map.138 = (bf16[128,512]{1,0:T(8,128)(2,1)}, f32[512,256]{1,0:T(8,128)}, f32[72,256]{1,0:T(8,128)}, f32[256,512]{1,0:T(8,128)}) custom-call(bf16[128,512]{1,0:T(8,128)(2,1)} %bitcast.11, bf16[128,512]{1,0:T(8,128)(2,1)} %bitcast.12, bf16[512,256]{1,0:T(8,128)(2,1)} %refs_2_.1, bf16[72,256]{1,0:T(8,128)(2,1)} %bitcast.13, bf16[256,512]{1,0:T(8,128)(2,1)} %refs_4_.1, ...), custom_call_target="tpu_custom_call" | custom-call | tf_op jit(solution)/shard_map/pallas_call | solution.py:463
  31.0 2.2 %shard_map.139 = (bf16[128,512]{1,0:T(8,128)(2,1)}, f32[512,256]{1,0:T(8,128)}, f32[72,256]{1,0:T(8,128)}, f32[256,512]{1,0:T(8,128)}) custom-call(bf16[128,512]{1,0:T(8,128)(2,1)} %get-tuple-element.12.refs_0_, f32[512,256]{1,0:T(8,128)} %get-tuple-element.13.refs_1_, f32[72,256]{1,0:T(8,128)} %get-tuple-element.14.refs_2_, ...), custom_call_target="tpu_custom_call" | custom-call | tf_op jit(solution)/shard_map/pallas_call | solution.py:502
